TPU v7x, 256 devices: a whole 4x4x8 slice. The times are simulated.
256 devices in a mesh: section: 64 (over z, y, core), rep: 4 (over x).
Axes of the slice: x: 4, y: 4, z: 8, core: 2. Of those that a mesh axis runs over, the one named last changes fastest.
Arguments:
- document_token_embedding: bfloat16 [8, 128, 4096], P('rep'), may hold values from -6 to 6
- doc_lengths: int32 [8, 4], P('rep'), may hold values from 1 to 32, as said below
- docid_embed: bfloat16 [8, 32, 4096], P('rep'), may hold values from -6 to 6
- docid_targets: int32 [8, 32], P('rep'), may hold values from 0 to 16383
- enc_gain: float32 [5, 4096], replicated, may hold values from 0.1 to 1.9
- dec_gain: float32 [2, 4096], replicated, may hold values from 0.1 to 1.9
- w_enc_qkv: bfloat16 [3, 12288, 4096], P(None, 'section'), may hold values from -0.03125 to 0.03125
- w_enc_out: bfloat16 [12288, 4096], P('section'), may hold values from -0.75 to 0.75
- cross_query_key_value_weight: bfloat16 [3, 4096, 4096], P(None, 'section'), may hold values from -0.03125 to 0.03125
- w_cross_out: bfloat16 [4096, 4096], P('section'), may hold values from -0.75 to 0.75
- docid_head_weight: bfloat16 [4096, 16384], P(None, 'section'), may hold values from -0.25 to 0.25
Outputs:
- logits: bfloat16 [8, 32, 16384], P('rep', None, 'section')
- token_loss: float32 [8, 32], P('rep')
- mean_loss: float32 [], replicated
Inputs may be any that keep to these rules, and one draw needn't show every extreme that they name: `doc_lengths`: in every draw some document has exactly 32 tokens.
All inputs are finite; a program needn't handle non-finite values.
Results may differ from a plain program's by a relative error of at most 0.019.
Values may be sent and summed in bfloat16 or wider, within the bound.
No kernel may reach another device: no remote copies, remote signals or barrier semaphores. Data moves between devices by JAX's collectives and lax.ppermute only.
A program may use at most 64 MiB of HBM per device.

v0:
```python
import jax
import jax.numpy as jnp
from jax import lax
from jax.sharding import PartitionSpec as P

HD = 64
GROUPS = 4


def from_partner(block, axis, distance):
    count = lax.axis_size(axis)
    route = []
    for low in range(count):
        high = low | 1 << distance
        if high != low and high < count:
            route += [(low, high), (high, low)]
    return lax.ppermute(block, axis, route)


def from_behind(block, axis, distance):
    devices = range(lax.axis_size(axis))
    route = [(i - distance, i) for i in devices if i - distance in devices]
    return lax.ppermute(block, axis, route)


def passed_along(shard, axis, by):
    size = lax.axis_size(axis)
    return lax.ppermute(shard, axis, [(i, (i + by) % size) for i in range(size)])


def cut_along(shard, dim, size):
    dims = shard.shape
    parts = shard.reshape(*dims[:dim], size, dims[dim] // size, *dims[dim + 1 :])
    return jnp.moveaxis(parts, dim, 0)


def summed_on_arrival(shard, axis, dim):
    size = lax.axis_size(axis)
    parts = lax.all_to_all(cut_along(shard, dim, size), axis, 0, 0, tiled=True)
    return jnp.sum(parts, axis=0)


def copy_for_each(shard, axis):
    size = lax.axis_size(axis)
    return lax.all_to_all(
        jnp.broadcast_to(shard[None], (size, *shard.shape)), axis, 0, 0, tiled=True
    )


def taken_together(shard, axis):
    everything = copy_for_each(shard, axis)
    return jnp.sum(everything, axis=0)


def together(arrays, axis):
    ends = [0]
    for a in arrays:
        ends.append(ends[-1] + a.size)
    running = taken_together(jnp.concatenate([a.ravel() for a in arrays]), axis)
    return tuple((running[b:e].reshape(a.shape) for a, b, e in zip(arrays, ends, ends[1:])))


def norm_rows(values, gain):
    values = values.astype(jnp.float32)
    scale = lax.rsqrt(jnp.mean(values * values, axis=-1, keepdims=True) + 1e-06)
    return values * scale * gain


def attend(queries, key_rows, values, allowed):
    scores = jnp.einsum("qhe,khe->hqk", queries, key_rows, preferred_element_type=jnp.float32)
    attention_weight_rows = jnp.where(allowed[None], jnp.exp(scores), 0.0)
    probabilities = (
        attention_weight_rows / jnp.sum(attention_weight_rows, axis=-1, keepdims=True)
    ).astype(jnp.bfloat16)
    mixture = jnp.einsum("hqk,khe->qhe", probabilities, values, preferred_element_type=jnp.float32)
    return mixture.astype(jnp.bfloat16)


def live_keys(lengths, key_doc, key_place):
    owners = jnp.arange(lengths.shape[0])
    matches = (key_doc[:, None] == owners[None, :]) & (key_place[:, None] < lengths[None, :])
    return jnp.any(matches, axis=1)


def lane_gather(own_rows, lane_bits, lane_index, concat_dim):
    for bit_number in range(lane_bits):
        partner = from_partner(own_rows, "section", bit_number)
        lower_half = lane_index // (1 << bit_number) % 2 == 0
        own_rows = jnp.where(
            lower_half,
            jnp.concatenate([own_rows, partner], concat_dim),
            jnp.concatenate([partner, own_rows], concat_dim),
        )
    return own_rows


def lane_reduce(totals, lane_bits, lane_index):
    for bit_number in reversed(range(lane_bits)):
        half_rows = totals.shape[0] // 2
        lower_half = lane_index // (1 << bit_number) % 2 == 0
        kept_rows = jnp.where(lower_half, totals[:half_rows], totals[half_rows:])
        outgoing = jnp.where(lower_half, totals[half_rows:], totals[:half_rows])
        totals = kept_rows + from_partner(
            outgoing.astype(jnp.bfloat16), "section", bit_number
        ).astype(outgoing.dtype)
    return totals


def relay_memory(encoder_memory, group_index, lane_count):
    encoder_memory = jnp.where(group_index == 0, encoder_memory, jnp.zeros_like(encoder_memory))
    for stride in (1, 2):
        encoder_memory = encoder_memory + from_behind(
            encoder_memory, "section", stride * lane_count
        )
    return encoder_memory


def shards(
    document_token_embedding,
    doc_lengths,
    docid_embed,
    docid_targets,
    enc_gain,
    dec_gain,
    w_enc_qkv,
    w_enc_out,
    cross_query_key_value_weight,
    w_cross_out,
    docid_head_weight,
):
    lane_count = lax.axis_size("section") // GROUPS
    lane_bits = lane_count.bit_length() - 1
    section_index = lax.axis_index("section")
    group_index = section_index // lane_count
    lane_index = section_index % lane_count
    micro_count, row_count, model_width = document_token_embedding.shape
    doc_count = doc_lengths.shape[1]
    doc_span = row_count // doc_count
    block_rows = row_count // lane_count
    local_heads = w_enc_qkv.shape[1] // HD
    positions = jnp.arange(row_count)
    key_doc = positions // doc_span
    key_place = positions % doc_span
    same_doc = key_doc[:, None] == key_doc[None, :]

    def partial_update(normed, lengths):
        allowed = same_doc & live_keys(lengths, key_doc, key_place)[None, :]
        projected = jnp.einsum(
            "rd,mcd->mrc", normed, w_enc_qkv, preferred_element_type=jnp.float32
        ).astype(jnp.bfloat16)
        projected = projected.reshape(3, row_count, local_heads, HD)
        mixture = attend(projected[0], projected[1], projected[2], allowed).reshape(row_count, -1)
        return jnp.dot(mixture, w_enc_out, preferred_element_type=jnp.float32)

    def section_step(step_index, loop_state):
        handed, encoder_memory = loop_state
        micro_index = step_index - group_index
        slot_index = jnp.clip(micro_index, 0, micro_count - 1)
        lengths = lax.dynamic_index_in_dim(doc_lengths, slot_index, 0, keepdims=False)
        layer_gain = lax.dynamic_index_in_dim(enc_gain, group_index, 0, keepdims=False)
        incoming = lax.dynamic_index_in_dim(
            document_token_embedding, jnp.minimum(step_index, micro_count - 1), 0, keepdims=False
        )
        incoming = lax.dynamic_slice_in_dim(incoming, lane_index * block_rows, block_rows, 0)
        current = jnp.where(group_index == 0, incoming, handed)
        normed = lane_gather(
            norm_rows(current, layer_gain).astype(jnp.bfloat16), lane_bits, lane_index, 0
        )
        summed = lane_reduce(partial_update(normed, lengths), lane_bits, lane_index)
        result = (current.astype(jnp.float32) + summed).astype(jnp.bfloat16)
        handed = passed_along(result, "section", lane_count)
        finished_index = step_index - (GROUPS - 1)
        finished_slot = jnp.clip(finished_index, 0, micro_count - 1)
        keeping = (group_index == 0) & (finished_index >= 0) & (finished_index < micro_count)
        stored = lax.dynamic_update_index_in_dim(encoder_memory, handed, finished_slot, 0)
        encoder_memory = jnp.where(keeping, stored, encoder_memory)
        return (handed, encoder_memory)

    handed = jnp.zeros((block_rows, model_width), jnp.bfloat16)
    encoder_memory = jnp.zeros((micro_count, block_rows, model_width), jnp.bfloat16)
    handed, encoder_memory = lax.fori_loop(
        0, micro_count + GROUPS - 1, section_step, (handed, encoder_memory)
    )
    encoder_memory = norm_rows(encoder_memory, enc_gain[GROUPS]).astype(jnp.bfloat16)
    encoder_memory = relay_memory(encoder_memory, group_index, lane_count)
    encoder_memory = lane_gather(encoder_memory, lane_bits, lane_index, 1)
    decoder_rows = docid_embed.shape[1]
    docid_span = decoder_rows // doc_count
    decoder_doc = jnp.arange(decoder_rows) // docid_span
    cross_heads = cross_query_key_value_weight.shape[1] // HD
    dec_normed = norm_rows(docid_embed, dec_gain[0]).astype(jnp.bfloat16)
    queries = jnp.einsum(
        "brd,cd->brc",
        dec_normed,
        cross_query_key_value_weight[0],
        preferred_element_type=jnp.float32,
    ).astype(jnp.bfloat16)
    memory_heads = jnp.einsum(
        "pye,qve->qpyv",
        encoder_memory,
        cross_query_key_value_weight[1:],
        preferred_element_type=jnp.float32,
    ).astype(jnp.bfloat16)

    def cross_one(sample_queries, sample_keys, sample_values, lengths):
        allowed = (decoder_doc[:, None] == key_doc[None, :]) & live_keys(
            lengths, key_doc, key_place
        )[None, :]
        return attend(sample_queries, sample_keys, sample_values, allowed)

    mixture = jax.vmap(cross_one)(
        queries.reshape(micro_count, decoder_rows, cross_heads, HD),
        memory_heads[0].reshape(micro_count, row_count, cross_heads, HD),
        memory_heads[1].reshape(micro_count, row_count, cross_heads, HD),
        doc_lengths,
    )
    cross_terms = jnp.einsum(
        "brc,cd->brd",
        mixture.reshape(micro_count, decoder_rows, -1),
        w_cross_out,
        preferred_element_type=jnp.float32,
    )
    share_rows = micro_count * decoder_rows // lax.axis_size("section")
    shared = summed_on_arrival(
        cross_terms.reshape(micro_count * decoder_rows, model_width), "section", 0
    )
    own_part = lax.dynamic_slice_in_dim(
        docid_embed.reshape(micro_count * decoder_rows, model_width),
        section_index * share_rows,
        share_rows,
        0,
    )
    normed_share = norm_rows(own_part.astype(jnp.float32) + shared, dec_gain[1]).astype(
        jnp.bfloat16
    )
    closing_rows = lax.all_gather(normed_share, "section", axis=0, tiled=True).reshape(
        micro_count, decoder_rows, model_width
    )
    scores_vocab = jnp.einsum(
        "brd,dv->brv", closing_rows, docid_head_weight, preferred_element_type=jnp.float32
    )
    vocab_local = docid_head_weight.shape[1]
    vocab_start = section_index * vocab_local
    matches = docid_targets[..., None] == vocab_start + jnp.arange(vocab_local)
    exponent_total, picked = together(
        (
            jnp.sum(jnp.exp(scores_vocab), axis=-1),
            jnp.sum(jnp.where(matches, scores_vocab, 0.0), axis=-1),
        ),
        "section",
    )
    token_loss = jnp.log(exponent_total) - picked
    mean_loss = lax.psum(jnp.sum(token_loss), "rep") / (token_loss.size * lax.axis_size("rep"))
    return (scores_vocab.astype(jnp.bfloat16), token_loss, mean_loss)


def solution(mesh):
    in_specs = (
        P("rep", None, None),
        P("rep", None),
        P("rep", None, None),
        P("rep", None),
        P(),
        P(),
        P(None, "section", None),
        P("section", None),
        P(None, "section", None),
        P("section", None),
        P(None, "section"),
    )
    out_specs = (P("rep", None, "section"), P("rep", None), P())
    return jax.shard_map(shards, mesh=mesh, in_specs=in_specs, out_specs=out_specs, check_vma=False)
```

profile of v0, /device:TPU:8, one launch (start us, length us, event | category | flops | bytes accessed | tf_op | source)
XLA Modules:
  0.0 559.5 jit_solution(2738783211067935834)
XLA Ops:
  2.0 356.9 %while.20 = (s32[]{:T(128)}, bf16[8,4096]{1,0:T(8,128)(2,1)S(1)}, bf16[2,8,4096]{2,1,0:T(8,128)(2,1)S(1)}, pred[]{:T(512)}, bf16[2,128,4096]{2,1,0:T(8,128)(2,1)...) while((s32[]{:T(128)}, bf16[8,4096]{1,0:T(8,128)(2,1)S(1)}, ...), condition=%wide.region_4.5_spmd.clone, body=%wide.region_0.4_spmd.clone.sunk | while | flops 829378432 | bytes 30887708 | solution.py:181
  12.7 7.5 %collective-permute-done.2 = bf16[32,4096]{1,0:T(8,128)(2,1)S(1)} collective-permute-done((bf16[32,4096]{1,0:T(8,128)(2,1)S(1)}, bf16[32,4096]{1,0:T(8,128)(2,1)S(1)}, u32[]{:S(2)}, u32[]{:S(2)}) %collective-permute-start.2) | collective-permute-done | bytes 262176 | tf_op jit(solution)/shard_map/while/body/eval_jaxpr/ppermute | solution.py:17
  21.7 11.2 %collective-permute-done.3 = bf16[64,4096]{1,0:T(8,128)(2,1)S(1)} collective-permute-done((bf16[64,4096]{1,0:T(8,128)(2,1)S(1)}, bf16[64,4096]{1,0:T(8,128)(2,1)S(1)}, u32[]{:S(2)}, u32[]{:S(2)}) %collective-permute-start.3) | collective-permute-done | bytes 524320 | tf_op jit(solution)/shard_map/while/body/eval_jaxpr/ppermute | solution.py:17
  40.0 10.8 %collective-permute-done.4 = bf16[64,4096]{1,0:T(8,128)(2,1)S(1)} collective-permute-done((bf16[64,4096]{1,0:T(8,128)(2,1)S(1)}, bf16[64,4096]{1,0:T(8,128)(2,1)S(1)}, u32[]{:S(2)}, u32[]{:S(2)}) %collective-permute-start.4) | collective-permute-done | bytes 524320 | tf_op jit(solution)/shard_map/while/body/eval_jaxpr/ppermute | solution.py:17
  52.3 8.0 %collective-permute-done.5 = bf16[32,4096]{1,0:T(8,128)(2,1)S(1)} collective-permute-done((bf16[32,4096]{1,0:T(8,128)(2,1)S(1)}, bf16[32,4096]{1,0:T(8,128)(2,1)S(1)}, u32[]{:S(2)}, u32[]{:S(2)}) %collective-permute-start.5) | collective-permute-done | bytes 262176 | tf_op jit(solution)/shard_map/while/body/eval_jaxpr/ppermute | solution.py:17
  68.4 5.4 collective-permute-done.8
  85.1 6.0 %collective-permute-done.2 = bf16[32,4096]{1,0:T(8,128)(2,1)S(1)} collective-permute-done((bf16[32,4096]{1,0:T(8,128)(2,1)S(1)}, bf16[32,4096]{1,0:T(8,128)(2,1)S(1)}, u32[]{:S(2)}, u32[]{:S(2)}) %collective-permute-start.2) | collective-permute-done | bytes 262176 | tf_op jit(solution)/shard_map/while/body/eval_jaxpr/ppermute | solution.py:17
  93.8 10.3 %collective-permute-done.3 = bf16[64,4096]{1,0:T(8,128)(2,1)S(1)} collective-permute-done((bf16[64,4096]{1,0:T(8,128)(2,1)S(1)}, bf16[64,4096]{1,0:T(8,128)(2,1)S(1)}, u32[]{:S(2)}, u32[]{:S(2)}) %collective-permute-start.3) | collective-permute-done | bytes 524320 | tf_op jit(solution)/shard_map/while/body/eval_jaxpr/ppermute | solution.py:17
  112.1 9.8 %collective-permute-done.4 = bf16[64,4096]{1,0:T(8,128)(2,1)S(1)} collective-permute-done((bf16[64,4096]{1,0:T(8,128)(2,1)S(1)}, bf16[64,4096]{1,0:T(8,128)(2,1)S(1)}, u32[]{:S(2)}, u32[]{:S(2)}) %collective-permute-start.4) | collective-permute-done | bytes 524320 | tf_op jit(solution)/shard_map/while/body/eval_jaxpr/ppermute | solution.py:17
  137.9 5.3 collective-permute-done.8
  155.7 5.8 %collective-permute-done.2 = bf16[32,4096]{1,0:T(8,128)(2,1)S(1)} collective-permute-done((bf16[32,4096]{1,0:T(8,128)(2,1)S(1)}, bf16[32,4096]{1,0:T(8,128)(2,1)S(1)}, u32[]{:S(2)}, u32[]{:S(2)}) %collective-permute-start.2) | collective-permute-done | bytes 262176 | tf_op jit(solution)/shard_map/while/body/eval_jaxpr/ppermute | solution.py:17
  164.5 10.6 %collective-permute-done.3 = bf16[64,4096]{1,0:T(8,128)(2,1)S(1)} collective-permute-done((bf16[64,4096]{1,0:T(8,128)(2,1)S(1)}, bf16[64,4096]{1,0:T(8,128)(2,1)S(1)}, u32[]{:S(2)}, u32[]{:S(2)}) %collective-permute-start.3) | collective-permute-done | bytes 524320 | tf_op jit(solution)/shard_map/while/body/eval_jaxpr/ppermute | solution.py:17
  183.1 10.1 %collective-permute-done.4 = bf16[64,4096]{1,0:T(8,128)(2,1)S(1)} collective-permute-done((bf16[64,4096]{1,0:T(8,128)(2,1)S(1)}, bf16[64,4096]{1,0:T(8,128)(2,1)S(1)}, u32[]{:S(2)}, u32[]{:S(2)}) %collective-permute-start.4) | collective-permute-done | bytes 524320 | tf_op jit(solution)/shard_map/while/body/eval_jaxpr/ppermute | solution.py:17
  196.2 5.2 collective-permute-done.5
  208.5 6.0 %collective-permute-done.8 = bf16[8,4096]{1,0:T(8,128)(2,1)S(1)} collective-permute-done((bf16[8,4096]{1,0:T(8,128)(2,1)S(1)}, bf16[8,4096]{1,0:T(8,128)(2,1)S(1)}, u32[]{:S(2)}, u32[]{:S(2)}) %collective-permute-start.8) | collective-permute-done | bytes 65568 | tf_op jit(solution)/shard_map/while/body/eval_jaxpr/ppermute | solution.py:28
  226.5 6.1 %collective-permute-done.2 = bf16[32,4096]{1,0:T(8,128)(2,1)S(1)} collective-permute-done((bf16[32,4096]{1,0:T(8,128)(2,1)S(1)}, bf16[32,4096]{1,0:T(8,128)(2,1)S(1)}, u32[]{:S(2)}, u32[]{:S(2)}) %collective-permute-start.2) | collective-permute-done | bytes 262176 | tf_op jit(solution)/shard_map/while/body/eval_jaxpr/ppermute | solution.py:17
  235.7 10.7 %collective-permute-done.3 = bf16[64,4096]{1,0:T(8,128)(2,1)S(1)} collective-permute-done((bf16[64,4096]{1,0:T(8,128)(2,1)S(1)}, bf16[64,4096]{1,0:T(8,128)(2,1)S(1)}, u32[]{:S(2)}, u32[]{:S(2)}) %collective-permute-start.3) | collective-permute-done | bytes 524320 | tf_op jit(solution)/shard_map/while/body/eval_jaxpr/ppermute | solution.py:17
  254.4 10.3 %collective-permute-done.4 = bf16[64,4096]{1,0:T(8,128)(2,1)S(1)} collective-permute-done((bf16[64,4096]{1,0:T(8,128)(2,1)S(1)}, bf16[64,4096]{1,0:T(8,128)(2,1)S(1)}, u32[]{:S(2)}, u32[]{:S(2)}) %collective-permute-start.4) | collective-permute-done | bytes 524320 | tf_op jit(solution)/shard_map/while/body/eval_jaxpr/ppermute | solution.py:17
  279.9 6.3 %collective-permute-done.8 = bf16[8,4096]{1,0:T(8,128)(2,1)S(1)} collective-permute-done((bf16[8,4096]{1,0:T(8,128)(2,1)S(1)}, bf16[8,4096]{1,0:T(8,128)(2,1)S(1)}, u32[]{:S(2)}, u32[]{:S(2)}) %collective-permute-start.8) | collective-permute-done | bytes 65568 | tf_op jit(solution)/shard_map/while/body/eval_jaxpr/ppermute | solution.py:28
  299.1 6.1 %collective-permute-done.2 = bf16[32,4096]{1,0:T(8,128)(2,1)S(1)} collective-permute-done((bf16[32,4096]{1,0:T(8,128)(2,1)S(1)}, bf16[32,4096]{1,0:T(8,128)(2,1)S(1)}, u32[]{:S(2)}, u32[]{:S(2)}) %collective-permute-start.2) | collective-permute-done | bytes 262176 | tf_op jit(solution)/shard_map/while/body/eval_jaxpr/ppermute | solution.py:17
  307.4 10.8 %collective-permute-done.3 = bf16[64,4096]{1,0:T(8,128)(2,1)S(1)} collective-permute-done((bf16[64,4096]{1,0:T(8,128)(2,1)S(1)}, bf16[64,4096]{1,0:T(8,128)(2,1)S(1)}, u32[]{:S(2)}, u32[]{:S(2)}) %collective-permute-start.3) | collective-permute-done | bytes 524320 | tf_op jit(solution)/shard_map/while/body/eval_jaxpr/ppermute | solution.py:17
  325.9 10.2 %collective-permute-done.4 = bf16[64,4096]{1,0:T(8,128)(2,1)S(1)} collective-permute-done((bf16[64,4096]{1,0:T(8,128)(2,1)S(1)}, bf16[64,4096]{1,0:T(8,128)(2,1)S(1)}, u32[]{:S(2)}, u32[]{:S(2)}) %collective-permute-start.4) | collective-permute-done | bytes 524320 | tf_op jit(solution)/shard_map/while/body/eval_jaxpr/ppermute | solution.py:17
  351.2 7.7 %collective-permute-done.8 = bf16[8,4096]{1,0:T(8,128)(2,1)S(1)} collective-permute-done((bf16[8,4096]{1,0:T(8,128)(2,1)S(1)}, bf16[8,4096]{1,0:T(8,128)(2,1)S(1)}, u32[]{:S(2)}, u32[]{:S(2)}) %collective-permute-start.8) | collective-permute-done | bytes 65568 | tf_op jit(solution)/shard_map/while/body/eval_jaxpr/ppermute | solution.py:28
  363.1 13.4 %collective-permute-start.10 = (bf16[2,8,4096]{2,1,0:T(8,128)(2,1)S(1)}, bf16[2,8,4096]{2,1,0:T(8,128)(2,1)S(1)}, u32[]{:S(2)}, u32[]{:S(2)}) collective-permute-start(bf16[2,8,4096]{2,1,0:T(8,128)(2,1)S(1)} %fusion.78), channel_id=1, source_target_pairs={{0,128},{4,132},{8,136},{12,140},{16,144},{20,148},{24,152},{28,15... | collective-permute-start | bytes 393224 | tf_op jit(solution)/shard_map/ppermute | solution.py:23
  382.4 6.6 %collective-permute-done.12 = bf16[2,16,4096]{2,1,0:T(8,128)(2,1)S(1)} collective-permute-done((bf16[2,16,4096]{2,1,0:T(8,128)(2,1)S(1)}, bf16[2,16,4096]{2,1,0:T(8,128)(2,1)S(1)}, u32[]{:S(2)}, u32[]{:S(2)}) %collective-permute-start.12) | collective-permute-done | bytes 262176 | tf_op jit(solution)/shard_map/ppermute | solution.py:17
  392.5 11.7 %collective-permute-done.13 = bf16[2,32,4096]{2,1,0:T(8,128)(2,1)S(1)} collective-permute-done((bf16[2,32,4096]{2,1,0:T(8,128)(2,1)S(1)}, bf16[2,32,4096]{2,1,0:T(8,128)(2,1)S(1)}, u32[]{:S(2)}, u32[]{:S(2)}) %collective-permute-start.13) | collective-permute-done | bytes 524320 | tf_op jit(solution)/shard_map/ppermute | solution.py:17
  406.7 21.9 %collective-permute-done.14 = bf16[2,64,4096]{2,1,0:T(8,128)(2,1)S(1)} collective-permute-done((bf16[2,64,4096]{2,1,0:T(8,128)(2,1)S(1)}, bf16[2,64,4096]{2,1,0:T(8,128)(2,1)S(1)}, u32[]{:S(2)}, u32[]{:S(2)}) %collective-permute-start.14) | collective-permute-done | bytes 1048608 | tf_op jit(solution)/shard_map/ppermute | solution.py:17
  433.6 12.6 %all-to-all-start = ((f32[64,1,4096]{2,1,0:T(1,128)}), f32[64,1,4096]{2,1,0:T(1,128)S(1)}, u32[]{:S(2)}, u32[]{:S(2)}) async-start(f32[64,1,4096]{2,1,0:T(1,128)} %copy.22), calls=%async_computation | async-start | bytes 2097152 | tf_op jit(solution)/shard_map/all_to_all | solution.py:39
  446.2 28.8 %all-to-all-done = f32[64,1,4096]{2,1,0:T(1,128)S(1)} async-done(((f32[64,1,4096]{2,1,0:T(1,128)}), f32[64,1,4096]{2,1,0:T(1,128)S(1)}, u32[]{:S(2)}, u32[]{:S(2)}) %all-to-all-start) | async-done | bytes 1048608 | tf_op jit(solution)/shard_map/all_to_all | solution.py:39
  479.0 48.6 %all-gather = bf16[64,1,4096]{2,1,0:T(2,128)(2,1)S(1)} all-gather(bf16[1,1,4096]{2,1,0:T(2,128)(2,1)S(1)} %convert_bitcast_fusion), channel_id=1, replica_groups=mesh['section'=64,'rep'=4] {'section'}, dimensions={0}, use_global_device_ids=true | all-gather | bytes 532480 | tf_op jit(solution)/shard_map/all_gather | solution.py:236
  529.5 15.6 %all_to_all.11 = f32[64,1,128]{2,1,0:T(1,128)S(1)} all-to-all(f32[64,1,128]{2,1,0:T(1,128)S(1)} %broadcast_in_dim.111), channel_id=1, replica_groups=mesh['section'=64,'rep'=4] {'section'}, dimensions={0} | all-to-all | bytes 65536 | tf_op jit(solution)/shard_map/all_to_all | solution.py:45
  545.8 11.3 %psum.7 = f32[]{:T(128)} all-reduce(f32[]{:T(128)} %get-tuple-element.917), channel_id=1, replica_groups=mesh['section'=64,'rep'=4] {'rep'}, use_global_device_ids=true, to_apply=%region_15.16 | all-reduce | flops 1 | bytes 8 | tf_op jit(solution)/shard_map/psum | solution.py:253
  (259 shorter events, 204.3 us)
Async XLA Ops:
  4.6 6.1 %collective-permute-start.1 = (bf16[16,4096]{1,0:T(8,128)(2,1)S(1)}, bf16[16,4096]{1,0:T(8,128)(2,1)S(1)}, u32[]{:S(2)}, u32[]{:S(2)}) collective-permute-start(bf16[16,4096]{1,0:T(8,128)(2,1)S(1)} %maximum_select_fusion.11), channel_id=1, source_target_pairs={{0,8},{8,0},{4,12},{12,4},{16,24},{24,16},{20,28},{28,20},{32,40},... | collective-permute-start | bytes 393224 | tf_op jit(solution)/shard_map/while/body/eval_jaxpr/ppermute | solution.py:17
  10.7 9.4 %collective-permute-start.2 = (bf16[32,4096]{1,0:T(8,128)(2,1)S(1)}, bf16[32,4096]{1,0:T(8,128)(2,1)S(1)}, u32[]{:S(2)}, u32[]{:S(2)}) collective-permute-start(bf16[32,4096]{1,0:T(8,128)(2,1)S(1)} %maximum_select_fusion.12), channel_id=1, source_target_pairs={{0,16},{16,0},{4,20},{20,4},{8,24},{24,8},{12,28},{28,12},{32,48},... | collective-permute-start | bytes 786440 | tf_op jit(solution)/shard_map/while/body/eval_jaxpr/ppermute | solution.py:17
  20.3 12.7 %collective-permute-start.3 = (bf16[64,4096]{1,0:T(8,128)(2,1)S(1)}, bf16[64,4096]{1,0:T(8,128)(2,1)S(1)}, u32[]{:S(2)}, u32[]{:S(2)}) collective-permute-start(bf16[64,4096]{1,0:T(8,128)(2,1)S(1)} %maximum_select_fusion.13), channel_id=1, source_target_pairs={{0,32},{32,0},{4,36},{36,4},{8,40},{40,8},{12,44},{44,12},{16,48},... | collective-permute-start | bytes 1572872 | tf_op jit(solution)/shard_map/while/body/eval_jaxpr/ppermute | solution.py:17
  39.1 11.7 %collective-permute-start.4 = (bf16[64,4096]{1,0:T(8,128)(2,1)S(1)}, bf16[64,4096]{1,0:T(8,128)(2,1)S(1)}, u32[]{:S(2)}, u32[]{:S(2)}) collective-permute-start(bf16[64,4096]{1,0:T(8,128)(2,1)S(1)} %select_convert_fusion.8), channel_id=1, source_target_pairs={{0,32},{32,0},{4,36},{36,4},{8,40},{40,8},{12,44},{44,12},{16,48},... | collective-permute-start | bytes 1572872 | tf_op jit(solution)/shard_map/while/body/eval_jaxpr/ppermute | solution.py:17
  51.0 9.4 %collective-permute-start.5 = (bf16[32,4096]{1,0:T(8,128)(2,1)S(1)}, bf16[32,4096]{1,0:T(8,128)(2,1)S(1)}, u32[]{:S(2)}, u32[]{:S(2)}) collective-permute-start(bf16[32,4096]{1,0:T(8,128)(2,1)S(1)} %select_convert_fusion.9), channel_id=1, source_target_pairs={{0,16},{16,0},{4,20},{20,4},{8,24},{24,8},{12,28},{28,12},{32,48},... | collective-permute-start | bytes 786440 | tf_op jit(solution)/shard_map/while/body/eval_jaxpr/ppermute | solution.py:17
  67.0 6.8 %collective-permute-start.8 = (bf16[8,4096]{1,0:T(8,128)(2,1)S(1)}, bf16[8,4096]{1,0:T(8,128)(2,1)S(1)}, u32[]{:S(2)}, u32[]{:S(2)}) collective-permute-start(bf16[8,4096]{1,0:T(8,128)(2,1)S(1)} %fusion.113), channel_id=1, source_target_pairs={{0,64},{4,68},{8,72},{12,76},{16,80},{20,84},{24,88},{28,92},{32,9... | collective-permute-start | bytes 196616 | tf_op jit(solution)/shard_map/while/body/eval_jaxpr/ppermute | solution.py:28
  82.1 9.1 %collective-permute-start.2 = (bf16[32,4096]{1,0:T(8,128)(2,1)S(1)}, bf16[32,4096]{1,0:T(8,128)(2,1)S(1)}, u32[]{:S(2)}, u32[]{:S(2)}) collective-permute-start(bf16[32,4096]{1,0:T(8,128)(2,1)S(1)} %maximum_select_fusion.12), channel_id=1, source_target_pairs={{0,16},{16,0},{4,20},{20,4},{8,24},{24,8},{12,28},{28,12},{32,48},... | collective-permute-start | bytes 786440 | tf_op jit(solution)/shard_map/while/body/eval_jaxpr/ppermute | solution.py:17
  91.3 12.8 %collective-permute-start.3 = (bf16[64,4096]{1,0:T(8,128)(2,1)S(1)}, bf16[64,4096]{1,0:T(8,128)(2,1)S(1)}, u32[]{:S(2)}, u32[]{:S(2)}) collective-permute-start(bf16[64,4096]{1,0:T(8,128)(2,1)S(1)} %maximum_select_fusion.13), channel_id=1, source_target_pairs={{0,32},{32,0},{4,36},{36,4},{8,40},{40,8},{12,44},{44,12},{16,48},... | collective-permute-start | bytes 1572872 | tf_op jit(solution)/shard_map/while/body/eval_jaxpr/ppermute | solution.py:17
  110.3 11.7 %collective-permute-start.4 = (bf16[64,4096]{1,0:T(8,128)(2,1)S(1)}, bf16[64,4096]{1,0:T(8,128)(2,1)S(1)}, u32[]{:S(2)}, u32[]{:S(2)}) collective-permute-start(bf16[64,4096]{1,0:T(8,128)(2,1)S(1)} %select_convert_fusion.8), channel_id=1, source_target_pairs={{0,32},{32,0},{4,36},{36,4},{8,40},{40,8},{12,44},{44,12},{16,48},... | collective-permute-start | bytes 1572872 | tf_op jit(solution)/shard_map/while/body/eval_jaxpr/ppermute | solution.py:17
  122.2 8.0 %collective-permute-start.5 = (bf16[32,4096]{1,0:T(8,128)(2,1)S(1)}, bf16[32,4096]{1,0:T(8,128)(2,1)S(1)}, u32[]{:S(2)}, u32[]{:S(2)}) collective-permute-start(bf16[32,4096]{1,0:T(8,128)(2,1)S(1)} %select_convert_fusion.9), channel_id=1, source_target_pairs={{0,16},{16,0},{4,20},{20,4},{8,24},{24,8},{12,28},{28,12},{32,48},... | collective-permute-start | bytes 786440 | tf_op jit(solution)/shard_map/while/body/eval_jaxpr/ppermute | solution.py:17
  136.7 6.5 %collective-permute-start.8 = (bf16[8,4096]{1,0:T(8,128)(2,1)S(1)}, bf16[8,4096]{1,0:T(8,128)(2,1)S(1)}, u32[]{:S(2)}, u32[]{:S(2)}) collective-permute-start(bf16[8,4096]{1,0:T(8,128)(2,1)S(1)} %fusion.113), channel_id=1, source_target_pairs={{0,64},{4,68},{8,72},{12,76},{16,80},{20,84},{24,88},{28,92},{32,9... | collective-permute-start | bytes 196616 | tf_op jit(solution)/shard_map/while/body/eval_jaxpr/ppermute | solution.py:28
  151.8 9.7 %collective-permute-start.2 = (bf16[32,4096]{1,0:T(8,128)(2,1)S(1)}, bf16[32,4096]{1,0:T(8,128)(2,1)S(1)}, u32[]{:S(2)}, u32[]{:S(2)}) collective-permute-start(bf16[32,4096]{1,0:T(8,128)(2,1)S(1)} %maximum_select_fusion.12), channel_id=1, source_target_pairs={{0,16},{16,0},{4,20},{20,4},{8,24},{24,8},{12,28},{28,12},{32,48},... | collective-permute-start | bytes 786440 | tf_op jit(solution)/shard_map/while/body/eval_jaxpr/ppermute | solution.py:17
  161.6 13.5 %collective-permute-start.3 = (bf16[64,4096]{1,0:T(8,128)(2,1)S(1)}, bf16[64,4096]{1,0:T(8,128)(2,1)S(1)}, u32[]{:S(2)}, u32[]{:S(2)}) collective-permute-start(bf16[64,4096]{1,0:T(8,128)(2,1)S(1)} %maximum_select_fusion.13), channel_id=1, source_target_pairs={{0,32},{32,0},{4,36},{36,4},{8,40},{40,8},{12,44},{44,12},{16,48},... | collective-permute-start | bytes 1572872 | tf_op jit(solution)/shard_map/while/body/eval_jaxpr/ppermute | solution.py:17
  181.2 12.0 %collective-permute-start.4 = (bf16[64,4096]{1,0:T(8,128)(2,1)S(1)}, bf16[64,4096]{1,0:T(8,128)(2,1)S(1)}, u32[]{:S(2)}, u32[]{:S(2)}) collective-permute-start(bf16[64,4096]{1,0:T(8,128)(2,1)S(1)} %select_convert_fusion.8), channel_id=1, source_target_pairs={{0,32},{32,0},{4,36},{36,4},{8,40},{40,8},{12,44},{44,12},{16,48},... | collective-permute-start | bytes 1572872 | tf_op jit(solution)/shard_map/while/body/eval_jaxpr/ppermute | solution.py:17
  193.4 8.0 %collective-permute-start.5 = (bf16[32,4096]{1,0:T(8,128)(2,1)S(1)}, bf16[32,4096]{1,0:T(8,128)(2,1)S(1)}, u32[]{:S(2)}, u32[]{:S(2)}) collective-permute-start(bf16[32,4096]{1,0:T(8,128)(2,1)S(1)} %select_convert_fusion.9), channel_id=1, source_target_pairs={{0,16},{16,0},{4,20},{20,4},{8,24},{24,8},{12,28},{28,12},{32,48},... | collective-permute-start | bytes 786440 | tf_op jit(solution)/shard_map/while/body/eval_jaxpr/ppermute | solution.py:17
  208.0 6.5 %collective-permute-start.8 = (bf16[8,4096]{1,0:T(8,128)(2,1)S(1)}, bf16[8,4096]{1,0:T(8,128)(2,1)S(1)}, u32[]{:S(2)}, u32[]{:S(2)}) collective-permute-start(bf16[8,4096]{1,0:T(8,128)(2,1)S(1)} %fusion.113), channel_id=1, source_target_pairs={{0,64},{4,68},{8,72},{12,76},{16,80},{20,84},{24,88},{28,92},{32,9... | collective-permute-start | bytes 196616 | tf_op jit(solution)/shard_map/while/body/eval_jaxpr/ppermute | solution.py:28
  223.0 9.6 %collective-permute-start.2 = (bf16[32,4096]{1,0:T(8,128)(2,1)S(1)}, bf16[32,4096]{1,0:T(8,128)(2,1)S(1)}, u32[]{:S(2)}, u32[]{:S(2)}) collective-permute-start(bf16[32,4096]{1,0:T(8,128)(2,1)S(1)} %maximum_select_fusion.12), channel_id=1, source_target_pairs={{0,16},{16,0},{4,20},{20,4},{8,24},{24,8},{12,28},{28,12},{32,48},... | collective-permute-start | bytes 786440 | tf_op jit(solution)/shard_map/while/body/eval_jaxpr/ppermute | solution.py:17
  232.7 13.8 %collective-permute-start.3 = (bf16[64,4096]{1,0:T(8,128)(2,1)S(1)}, bf16[64,4096]{1,0:T(8,128)(2,1)S(1)}, u32[]{:S(2)}, u32[]{:S(2)}) collective-permute-start(bf16[64,4096]{1,0:T(8,128)(2,1)S(1)} %maximum_select_fusion.13), channel_id=1, source_target_pairs={{0,32},{32,0},{4,36},{36,4},{8,40},{40,8},{12,44},{44,12},{16,48},... | collective-permute-start | bytes 1572872 | tf_op jit(solution)/shard_map/while/body/eval_jaxpr/ppermute | solution.py:17
  252.6 12.1 %collective-permute-start.4 = (bf16[64,4096]{1,0:T(8,128)(2,1)S(1)}, bf16[64,4096]{1,0:T(8,128)(2,1)S(1)}, u32[]{:S(2)}, u32[]{:S(2)}) collective-permute-start(bf16[64,4096]{1,0:T(8,128)(2,1)S(1)} %select_convert_fusion.8), channel_id=1, source_target_pairs={{0,32},{32,0},{4,36},{36,4},{8,40},{40,8},{12,44},{44,12},{16,48},... | collective-permute-start | bytes 1572872 | tf_op jit(solution)/shard_map/while/body/eval_jaxpr/ppermute | solution.py:17
  264.9 8.0 %collective-permute-start.5 = (bf16[32,4096]{1,0:T(8,128)(2,1)S(1)}, bf16[32,4096]{1,0:T(8,128)(2,1)S(1)}, u32[]{:S(2)}, u32[]{:S(2)}) collective-permute-start(bf16[32,4096]{1,0:T(8,128)(2,1)S(1)} %select_convert_fusion.9), channel_id=1, source_target_pairs={{0,16},{16,0},{4,20},{20,4},{8,24},{24,8},{12,28},{28,12},{32,48},... | collective-permute-start | bytes 786440 | tf_op jit(solution)/shard_map/while/body/eval_jaxpr/ppermute | solution.py:17
  279.5 6.7 %collective-permute-start.8 = (bf16[8,4096]{1,0:T(8,128)(2,1)S(1)}, bf16[8,4096]{1,0:T(8,128)(2,1)S(1)}, u32[]{:S(2)}, u32[]{:S(2)}) collective-permute-start(bf16[8,4096]{1,0:T(8,128)(2,1)S(1)} %fusion.113), channel_id=1, source_target_pairs={{0,64},{4,68},{8,72},{12,76},{16,80},{20,84},{24,88},{28,92},{32,9... | collective-permute-start | bytes 196616 | tf_op jit(solution)/shard_map/while/body/eval_jaxpr/ppermute | solution.py:28
  288.8 6.8 %collective-permute-start.1 = (bf16[16,4096]{1,0:T(8,128)(2,1)S(1)}, bf16[16,4096]{1,0:T(8,128)(2,1)S(1)}, u32[]{:S(2)}, u32[]{:S(2)}) collective-permute-start(bf16[16,4096]{1,0:T(8,128)(2,1)S(1)} %maximum_select_fusion.11), channel_id=1, source_target_pairs={{0,8},{8,0},{4,12},{12,4},{16,24},{24,16},{20,28},{28,20},{32,40},... | collective-permute-start | bytes 393224 | tf_op jit(solution)/shard_map/while/body/eval_jaxpr/ppermute | solution.py:17
  295.6 9.6 %collective-permute-start.2 = (bf16[32,4096]{1,0:T(8,128)(2,1)S(1)}, bf16[32,4096]{1,0:T(8,128)(2,1)S(1)}, u32[]{:S(2)}, u32[]{:S(2)}) collective-permute-start(bf16[32,4096]{1,0:T(8,128)(2,1)S(1)} %maximum_select_fusion.12), channel_id=1, source_target_pairs={{0,16},{16,0},{4,20},{20,4},{8,24},{24,8},{12,28},{28,12},{32,48},... | collective-permute-start | bytes 786440 | tf_op jit(solution)/shard_map/while/body/eval_jaxpr/ppermute | solution.py:17
  305.3 12.8 %collective-permute-start.3 = (bf16[64,4096]{1,0:T(8,128)(2,1)S(1)}, bf16[64,4096]{1,0:T(8,128)(2,1)S(1)}, u32[]{:S(2)}, u32[]{:S(2)}) collective-permute-start(bf16[64,4096]{1,0:T(8,128)(2,1)S(1)} %maximum_select_fusion.13), channel_id=1, source_target_pairs={{0,32},{32,0},{4,36},{36,4},{8,40},{40,8},{12,44},{44,12},{16,48},... | collective-permute-start | bytes 1572872 | tf_op jit(solution)/shard_map/while/body/eval_jaxpr/ppermute | solution.py:17
  324.3 11.9 %collective-permute-start.4 = (bf16[64,4096]{1,0:T(8,128)(2,1)S(1)}, bf16[64,4096]{1,0:T(8,128)(2,1)S(1)}, u32[]{:S(2)}, u32[]{:S(2)}) collective-permute-start(bf16[64,4096]{1,0:T(8,128)(2,1)S(1)} %select_convert_fusion.8), channel_id=1, source_target_pairs={{0,32},{32,0},{4,36},{36,4},{8,40},{40,8},{12,44},{44,12},{16,48},... | collective-permute-start | bytes 1572872 | tf_op jit(solution)/shard_map/while/body/eval_jaxpr/ppermute | solution.py:17
  336.4 8.1 %collective-permute-start.5 = (bf16[32,4096]{1,0:T(8,128)(2,1)S(1)}, bf16[32,4096]{1,0:T(8,128)(2,1)S(1)}, u32[]{:S(2)}, u32[]{:S(2)}) collective-permute-start(bf16[32,4096]{1,0:T(8,128)(2,1)S(1)} %select_convert_fusion.9), channel_id=1, source_target_pairs={{0,16},{16,0},{4,20},{20,4},{8,24},{24,8},{12,28},{28,12},{32,48},... | collective-permute-start | bytes 786440 | tf_op jit(solution)/shard_map/while/body/eval_jaxpr/ppermute | solution.py:17
  351.1 7.8 %collective-permute-start.8 = (bf16[8,4096]{1,0:T(8,128)(2,1)S(1)}, bf16[8,4096]{1,0:T(8,128)(2,1)S(1)}, u32[]{:S(2)}, u32[]{:S(2)}) collective-permute-start(bf16[8,4096]{1,0:T(8,128)(2,1)S(1)} %fusion.113), channel_id=1, source_target_pairs={{0,64},{4,68},{8,72},{12,76},{16,80},{20,84},{24,88},{28,92},{32,9... | collective-permute-start | bytes 196616 | tf_op jit(solution)/shard_map/while/body/eval_jaxpr/ppermute | solution.py:28
  363.1 15.9 %collective-permute-start.10 = (bf16[2,8,4096]{2,1,0:T(8,128)(2,1)S(1)}, bf16[2,8,4096]{2,1,0:T(8,128)(2,1)S(1)}, u32[]{:S(2)}, u32[]{:S(2)}) collective-permute-start(bf16[2,8,4096]{2,1,0:T(8,128)(2,1)S(1)} %fusion.78), channel_id=1, source_target_pairs={{0,128},{4,132},{8,136},{12,140},{16,144},{20,148},{24,152},{28,15... | collective-permute-start | bytes 393224 | tf_op jit(solution)/shard_map/ppermute | solution.py:23
  380.5 8.5 %collective-permute-start.12 = (bf16[2,16,4096]{2,1,0:T(8,128)(2,1)S(1)}, bf16[2,16,4096]{2,1,0:T(8,128)(2,1)S(1)}, u32[]{:S(2)}, u32[]{:S(2)}) collective-permute-start(bf16[2,16,4096]{2,1,0:T(8,128)(2,1)S(1)} %maximum_select_fusion.7), channel_id=1, source_target_pairs={{0,8},{8,0},{4,12},{12,4},{16,24},{24,16},{20,28},{28,20},{32,40},... | collective-permute-start | bytes 786440 | tf_op jit(solution)/shard_map/ppermute | solution.py:17
  389.1 15.1 %collective-permute-start.13 = (bf16[2,32,4096]{2,1,0:T(8,128)(2,1)S(1)}, bf16[2,32,4096]{2,1,0:T(8,128)(2,1)S(1)}, u32[]{:S(2)}, u32[]{:S(2)}) collective-permute-start(bf16[2,32,4096]{2,1,0:T(8,128)(2,1)S(1)} %maximum_select_fusion.6), channel_id=1, source_target_pairs={{0,16},{16,0},{4,20},{20,4},{8,24},{24,8},{12,28},{28,12},{32,48},... | collective-permute-start | bytes 1572872 | tf_op jit(solution)/shard_map/ppermute | solution.py:17
  404.4 24.1 %collective-permute-start.14 = (bf16[2,64,4096]{2,1,0:T(8,128)(2,1)S(1)}, bf16[2,64,4096]{2,1,0:T(8,128)(2,1)S(1)}, u32[]{:S(2)}, u32[]{:S(2)}) collective-permute-start(bf16[2,64,4096]{2,1,0:T(8,128)(2,1)S(1)} %maximum_select_fusion.5), channel_id=1, source_target_pairs={{0,32},{32,0},{4,36},{36,4},{8,40},{40,8},{12,44},{44,12},{16,48},... | collective-permute-start | bytes 3145736 | tf_op jit(solution)/shard_map/ppermute | solution.py:17
  433.6 41.4 %all-to-all-start = ((f32[64,1,4096]{2,1,0:T(1,128)}), f32[64,1,4096]{2,1,0:T(1,128)S(1)}, u32[]{:S(2)}, u32[]{:S(2)}) async-start(f32[64,1,4096]{2,1,0:T(1,128)} %copy.22), calls=%async_computation | async-start | bytes 2097152 | tf_op jit(solution)/shard_map/all_to_all | solution.py:39
  (33 other events, 978.0 us)
where the time goes:
time: 561 us; the launch traced here: 559 us
  waiting for transfers between devices  321 us (57%)
  starting transfers between devices  105 us (19%)
  blocking collectives  75.5 us (13%)
  matrix products  34.2 us (6%)
  other arithmetic  15.2 us (3%)
    ppermute x44, waiting for transfers between devices, from_partner(): return lax.ppermute(block, axis, route)  257 us
    ppermute x44, starting transfers between devices, from_partner(): return lax.ppermute(block, axis, route)  73.6 us
    all_gather x1, blocking collectives, shards(): lax.all_gather(normed_share, 'section', axis=0, tiled=True)  48.6 us
    ppermute x5, waiting for transfers between devices, passed_along(): lax.ppermute(shard, axis, [(i, (i + by) % size) for i in range(size)])  30.6 us
    all_to_all x1, waiting for transfers between devices, summed_on_arrival(): parts = lax.all_to_all(cut_along(shard, dim, size), axis, 0, 0, tiled=True)  28.8 us
    dot_general x5, matrix products, partial_update(): jnp.einsum('rd,mcd->mrc', normed, w_enc_qkv, preferred_element_type=jnp.f...  18.7 us
    all_to_all x1, blocking collectives, copy_for_each(): lax.all_to_all(jnp.broadcast_to(shard[None], (size, *shard.shape)), axis,...  15.6 us
    ppermute x2, starting transfers between devices, from_behind(): return lax.ppermute(block, axis, route)  14.7 us
  transfers between devices with their start and end apart: 52, of which 52 were waited for; matrix products, arithmetic and copies ran while one was open for 0% of the time, Pallas kernels for 0%

commit v1 on v0

v1 whole, which is shorter than its diff:
```python
import jax
import jax.numpy as jnp
from jax import lax
from jax.sharding import PartitionSpec as P

HD = 64
GROUPS = 4
LANES_Y = 4
CHAINS = 2


def routed(block, pairs):
    return lax.ppermute(block, "section", pairs)


def lanes_of(group):
    return range(group * 16, group * 16 + 16)


def swapped(block, group, mask):
    return routed(block, [(s, s ^ mask) for s in lanes_of(group)])


CORE, ROW, PLANE = 1, 2, 8


def norm_rows(values, gain):
    values = values.astype(jnp.float32)
    scale = lax.rsqrt(jnp.mean(values * values, axis=-1, keepdims=True) + 1e-06)
    return values * scale * gain


def attend(queries, key_rows, values, allowed):
    scores = jnp.einsum("qhe,khe->hqk", queries, key_rows, preferred_element_type=jnp.float32)
    weights = jnp.where(allowed[None], jnp.exp(scores), 0.0)
    probabilities = (weights / jnp.sum(weights, axis=-1, keepdims=True)).astype(jnp.bfloat16)
    mixture = jnp.einsum("hqk,khe->qhe", probabilities, values, preferred_element_type=jnp.float32)
    return mixture.astype(jnp.bfloat16)


def gather_rows(own, group):
    pair = jnp.concatenate([own, swapped(own, group, PLANE)], 0)
    ring = jnp.concatenate(
        [pair] + [swapped(pair, group, ROW * k) for k in range(1, LANES_Y)], 0
    )
    return jnp.concatenate([ring, swapped(ring, group, CORE)], 0)


def reduce_rows(mixture, weight, group):
    half = mixture.shape[0] // 2
    away = jnp.dot(mixture[half:], weight, preferred_element_type=jnp.float32)
    arrived = swapped(away.astype(jnp.bfloat16), group, CORE)
    own = jnp.dot(mixture[:half], weight, preferred_element_type=jnp.float32)
    ring = own + arrived.astype(jnp.float32)
    quarter = half // LANES_Y
    sent = ring.astype(jnp.bfloat16)
    pair = ring[:quarter]
    for k in range(1, LANES_Y):
        block = swapped(sent[k * quarter : (k + 1) * quarter], group, ROW * k)
        pair = pair + block.astype(jnp.float32)
    eighth = quarter // 2
    arrived = swapped(pair[eighth:].astype(jnp.bfloat16), group, PLANE)
    return pair[:eighth] + arrived.astype(jnp.float32)


def shards(
    document_token_embedding,
    doc_lengths,
    docid_embed,
    docid_targets,
    enc_gain,
    dec_gain,
    w_enc_qkv,
    w_enc_out,
    cross_query_key_value_weight,
    w_cross_out,
    docid_head_weight,
):
    section_index = lax.axis_index("section")
    core = section_index % 2
    ring_y = section_index // 2 % LANES_Y
    plane = section_index // 8 % 2
    micro_count, row_count, model_width = document_token_embedding.shape
    doc_count = doc_lengths.shape[1]
    doc_span = row_count // doc_count
    decoder_rows = docid_embed.shape[1]
    docid_span = decoder_rows // doc_count
    local_heads = w_enc_qkv.shape[1] // HD
    lanes = 16
    last = GROUPS - 1

    def order_of(span):
        rows = span // 4
        index = jnp.arange(doc_count * span)
        kc = index // (doc_count * span // 2)
        ky = index // (2 * rows) % LANES_Y
        kz = index // rows % 2
        doc = ring_y ^ ky
        place = ((plane ^ kz) * 2 + (core ^ kc)) * rows + index % rows
        return doc, place

    enc_doc, enc_place = order_of(doc_span)
    dec_doc, dec_place = order_of(docid_span)
    enc_order = enc_doc * doc_span + enc_place
    dec_order = dec_doc * docid_span + dec_place
    same_doc = enc_doc[:, None] == enc_doc[None, :]
    cross_doc = dec_doc[:, None] == enc_doc[None, :]

    lengths_there = [jnp.take(doc_lengths[m], enc_doc) for m in range(micro_count)]
    live = [enc_place < lengths_there[m] for m in range(micro_count)]
    allowed = [same_doc & live[m][None, :] for m in range(micro_count)]
    cross_allowed = [cross_doc & live[m][None, :] for m in range(micro_count)]

    docid_rows = jnp.take(docid_embed, dec_order, axis=1)
    dec_normed = norm_rows(docid_rows, dec_gain[0]).astype(jnp.bfloat16)
    own_queries = jnp.einsum(
        "brd,cd->brc",
        dec_normed,
        cross_query_key_value_weight[0],
        preferred_element_type=jnp.float32,
    ).astype(jnp.bfloat16)

    def to_last(block):
        pieces = [block]
        for k in range(1, GROUPS):
            pairs = [(s - k * lanes, s) for s in lanes_of(last)]
            pieces.append(routed(block, pairs))
        return pieces

    cross_queries = jnp.stack(to_last(own_queries), 2)
    cross_maps = jnp.concatenate(to_last(cross_query_key_value_weight[1:]), 1)
    cross_out = jnp.concatenate(to_last(w_cross_out), 0)

    def project(normed):
        return jnp.einsum(
            "rd,mcd->mrc", normed, w_enc_qkv, preferred_element_type=jnp.float32
        ).astype(jnp.bfloat16)

    def mix(normed, mask):
        projected = project(normed).reshape(3, row_count, local_heads, HD)
        return attend(projected[0], projected[1], projected[2], mask).reshape(row_count, -1)

    block_rows = row_count // lanes
    hidden = []
    for m in range(micro_count):
        rows = jnp.take(document_token_embedding[m], enc_order, axis=0)
        normed = norm_rows(rows, enc_gain[0]).astype(jnp.bfloat16)
        summed = reduce_rows(mix(normed, allowed[m]), w_enc_out, 0)
        hidden.append((rows[:block_rows].astype(jnp.float32) + summed).astype(jnp.bfloat16))
    for group in range(1, GROUPS):
        for m in range(micro_count):
            own = routed(hidden[m], [(s - lanes, s) for s in lanes_of(group)])
            normed = gather_rows(norm_rows(own, enc_gain[group]).astype(jnp.bfloat16), group)
            summed = reduce_rows(mix(normed, allowed[m]), w_enc_out, group)
            hidden[m] = (own.astype(jnp.float32) + summed).astype(jnp.bfloat16)

    mixtures = []
    for m in range(micro_count):
        memory = gather_rows(norm_rows(hidden[m], enc_gain[GROUPS]).astype(jnp.bfloat16), last)
        heads = jnp.einsum(
            "rd,qcd->qrc", memory, cross_maps, preferred_element_type=jnp.float32
        ).astype(jnp.bfloat16)
        heads = heads.reshape(2, row_count, GROUPS, HD)
        mixtures.append(
            attend(cross_queries[m], heads[0], heads[1], cross_allowed[m]).reshape(
                decoder_rows, -1
            )
        )
    share = docid_span // 4

    def interleaved(pieces):
        stacked = jnp.stack([p.reshape(lanes, share, -1) for p in pieces], 1)
        return stacked.reshape(lanes * micro_count * share, -1)

    own_docid = jnp.concatenate([docid_rows[m, :share] for m in range(micro_count)], 0)
    cross_sum = reduce_rows(interleaved(mixtures), cross_out, last)
    final_own = norm_rows(own_docid.astype(jnp.float32) + cross_sum, dec_gain[1]).astype(
        jnp.bfloat16
    )
    other = swapped(final_own, last, PLANE)
    first_half = jnp.where(plane == 0, final_own, other)
    second_half = jnp.where(plane == 0, other, final_own)
    final_pair = jnp.concatenate([first_half, second_half], 0)
    depth = section_index // 8
    for step, (up, down) in enumerate((((7, 0), (6, 5)), ((0, 1), (5, 4)), ((1, 2), (4, 3)))):
        pairs = [(up[0] * 8 + s, up[1] * 8 + s) for s in range(8)]
        pairs += [(down[0] * 8 + s, down[1] * 8 + s) for s in range(8)]
        arrived = routed(final_pair, pairs)
        final_pair = jnp.where((depth == up[1]) | (depth == down[1]), arrived, final_pair)
    everyone = range(64)
    ring = jnp.concatenate(
        [final_pair]
        + [
            routed(final_pair, [(s, s ^ (ROW * k)) for s in everyone]) for k in range(1, LANES_Y)
        ],
        0,
    )
    closing = jnp.concatenate([ring, routed(ring, [(s, s ^ CORE) for s in everyone])], 0)

    scores_here = jnp.dot(closing, docid_head_weight, preferred_element_type=jnp.float32)
    vocab_local = docid_head_weight.shape[1]
    index = jnp.arange(micro_count * decoder_rows)
    micro = index // decoder_rows
    doc = index // docid_span % doc_count
    place = index % docid_span
    half, quarter, row = place // (2 * share), place // share % 2, place % share
    source = ((((quarter ^ core) * LANES_Y + (doc ^ ring_y)) * 2 + half) * micro_count + micro)
    scores_vocab = jnp.take(scores_here, source * share + row, axis=0).reshape(
        micro_count, decoder_rows, vocab_local
    )
    vocab_start = section_index * vocab_local
    matches = docid_targets[..., None] == vocab_start + jnp.arange(vocab_local)
    parts = jnp.stack(
        [
            jnp.sum(jnp.exp(scores_vocab), axis=-1),
            jnp.sum(jnp.where(matches, scores_vocab, 0.0), axis=-1),
        ]
    ).reshape(1, -1)
    size = lax.axis_size("section")
    everything = lax.all_to_all(
        jnp.broadcast_to(parts[None], (size, *parts.shape)), "section", 0, 0, tiled=True
    )
    exponent_total, picked = jnp.sum(everything, axis=0).reshape(
        2, micro_count, decoder_rows
    )
    token_loss = jnp.log(exponent_total) - picked
    total = jnp.sum(token_loss).reshape(1, 1)
    for mask in (1, 3):
        total = total + lax.ppermute(total, "rep", [(i, i ^ mask) for i in range(4)])
    mean_loss = total[0, 0] / (token_loss.size * lax.axis_size("rep"))
    return (scores_vocab.astype(jnp.bfloat16), token_loss, mean_loss)


def solution(mesh):
    in_specs = (
        P("rep", None, None),
        P("rep", None),
        P("rep", None, None),
        P("rep", None),
        P(),
        P(),
        P(None, "section", None),
        P("section", None),
        P(None, "section", None),
        P("section", None),
        P(None, "section"),
    )
    out_specs = (P("rep", None, "section"), P("rep", None), P())
    return jax.shard_map(shards, mesh=mesh, in_specs=in_specs, out_specs=out_specs, check_vma=False)
```

time: 561 us -> 701 us (1.25); the launches traced: 559 us -> 689 us
  starting transfers between devices: 105 us -> 455 us
  waiting for transfers between devices: 321 us -> 96.9 us
  blocking collectives: 75.5 us -> 0 us
  matrix products: 34.2 us -> 73.2 us
  local copies, waits for them, and re-layouts: 4.78 us -> 38.8 us
    ppermute x51 -> x110, starting transfers between devices: 92 us -> 443 us  [the longest x108 425 us: routed(): return lax.ppermute(block, 'section', pairs)]
    ppermute x51 -> x110, waiting for transfers between devices: 292 us -> 89 us  [the longest x108 83.1 us: routed(): return lax.ppermute(block, 'section', pairs)]
    all_gather x1 -> x0, blocking collectives: 48.6 us -> none  [shards(): lax.all_gather(normed_share, 'section', axis=0, tiled=True)]
    dot_general x13 -> x30, matrix products: 30.3 us -> 63.2 us  [the longest x8 23.3 us: project(): jnp.einsum('rd,mcd->mrc', normed, w_enc_qkv, preferred_element_type=jnp.f...]
    all_to_all x1, waiting for transfers between devices: 28.8 us -> 7.91 us  [shards(): lax.all_to_all(jnp.broadcast_to(parts[None], (size, *parts.shape)), 'sect...]
    all_to_all x1 -> x0, blocking collectives: 15.6 us -> none  [copy_for_each(): lax.all_to_all(jnp.broadcast_to(shard[None], (size, *shard.shape)), axis,...]
    psum x1 -> x0, blocking collectives: 11.3 us -> none  [shards(): lax.psum(jnp.sum(token_loss), 'rep')]
    gather x0 -> x6, local copies, waits for them, and re-layouts: none -> 11.2 us  [the longest x2 6.72 us: shards(): rows = jnp.take(document_token_embedding[m], enc_order, axis=0)]
  transfers between devices with their start and end apart: 52 -> 111, of which waited for: 52 -> 14; matrix products, arithmetic and copies ran while one was open for 0% -> 16% of each run, Pallas kernels for 0% -> 0%
where the time goes in v1:
time: 701 us; the launch traced here: 689 us
  starting transfers between devices  455 us (65%)
  waiting for transfers between devices  96.9 us (14%)
  matrix products  73.2 us (10%)
  local copies, waits for them, and re-layouts  38.8 us (6%)
  other arithmetic  17.9 us (3%)
  between operations  7.29 us (1%)
    ppermute x108, starting transfers between devices, routed(): return lax.ppermute(block, 'section', pairs)  425 us
    ppermute x108, waiting for transfers between devices, routed(): return lax.ppermute(block, 'section', pairs)  83.1 us
    dot_general x8, matrix products, project(): jnp.einsum('rd,mcd->mrc', normed, w_enc_qkv, preferred_element_type=jnp.f...  23.3 us
    dot_general x9, matrix products, reduce_rows(): away = jnp.dot(mixture[half:], weight, preferred_element_type=jnp.float32)  20.6 us
    ppermute x2, starting transfers between devices, shards(): lax.ppermute(total, 'rep', [(i, i ^ mask) for i in range(4)])  18.3 us
  transfers between devices with their start and end apart: 111, of which 14 were waited for; matrix products, arithmetic and copies ran while one was open for 16% of the time, Pallas kernels for 0%

profile of v1, /device:TPU:8, one launch (start us, length us, event | category | flops | bytes accessed | tf_op | source)
XLA Modules:
  0.0 688.8 jit_solution(11660858753609402014)
XLA Ops:
  7.0 8.8 %collective-permute-start.48 = (bf16[2,32,64]{2,1,0:T(8,128)(2,1)S(1)}, bf16[2,32,64]{2,1,0:T(8,128)(2,1)}, u32[]{:S(2)}, u32[]{:S(2)}) collective-permute-start(bf16[2,32,64]{2,1,0:T(8,128)(2,1)S(1)} %convolution_convert_fusion.29), channel_id=1, source_target_pairs={{0,192},{4,196},{8,200},{12,204},{16,208},{20,212},{24,216},{28,22... | collective-permute-start | bytes 24584 | tf_op jit(solution)/shard_map/ppermute | solution.py:13
  23.4 4.5 gather_fusion.3
  30.1 2.9 fusion.3
  33.0 4.2 fusion.18
  51.0 3.8 fusion.14
  60.0 8.9 %collective-permute-start.1 = (bf16[2,64,4096]{2,1,0:T(8,128)(2,1)}, bf16[2,64,4096]{2,1,0:T(8,128)(2,1)}, u32[]{:S(2)}, u32[]{:S(2)}) collective-permute-start(bf16[2,64,4096]{2,1,0:T(8,128)(2,1)} %slice.457), channel_id=1, source_target_pairs={{64,192},{68,196},{72,200},{76,204},{80,208},{84,212},{88,216},{92... | collective-permute-start | bytes 3145736 | tf_op jit(solution)/shard_map/ppermute | solution.py:13
  74.9 5.7 collective-permute-start.94
  81.1 3.6 collective-permute-start.52
  84.7 2.9 collective-permute-start.51
  87.7 62.9 %collective-permute-done.94 = bf16[64,4096]{1,0:T(8,128)(2,1)S(1)} collective-permute-done((bf16[64,4096]{1,0:T(8,128)(2,1)S(1)}, bf16[64,4096]{1,0:T(8,128)(2,1)S(1)}, u32[]{:S(2)}, u32[]{:S(2)}) %collective-permute-start.94) | collective-permute-done | bytes 524320 | tf_op jit(solution)/shard_map/ppermute | solution.py:13
  153.1 4.3 collective-permute-start.6
  157.4 3.1 collective-permute-start.5
  197.2 3.7 fusion.15
  212.2 57.5 %collective-permute-start.65 = (bf16[8,4096]{1,0:T(8,128)(2,1)S(1)}, bf16[8,4096]{1,0:T(8,128)(2,1)S(1)}, u32[]{:S(2)}, u32[]{:S(2)}) collective-permute-start(bf16[8,4096]{1,0:T(8,128)(2,1)S(1)} %fusion.97), channel_id=1, source_target_pairs={{64,128},{68,132},{72,136},{76,140},{80,144},{84,148},{88,152},{92... | collective-permute-start | bytes 196616 | tf_op jit(solution)/shard_map/ppermute | solution.py:13
  269.7 12.5 %collective-permute-start.19 = (bf16[8,4096]{1,0:T(8,128)(2,1)S(1)}, bf16[8,4096]{1,0:T(8,128)(2,1)S(1)}, u32[]{:S(2)}, u32[]{:S(2)}) collective-permute-start(bf16[8,4096]{1,0:T(8,128)(2,1)S(1)} %fusion.85), channel_id=1, source_target_pairs={{64,128},{68,132},{72,136},{76,140},{80,144},{84,148},{88,152},{92... | collective-permute-start | bytes 196616 | tf_op jit(solution)/shard_map/ppermute | solution.py:13
  302.9 3.7 fusion.16
  339.8 3.7 fusion.17
  366.3 3.2 fusion.22
  370.9 3.7 fusion.23
  384.8 175.6 %collective-permute-start.101 = (bf16[8,4096]{1,0:T(8,128)(2,1)S(1)}, bf16[8,4096]{1,0:T(8,128)(2,1)S(1)}, u32[]{:S(2)}, u32[]{:S(2)}) collective-permute-start(bf16[8,4096]{1,0:T(8,128)(2,1)S(1)} %pad_maximum_fusion.13), channel_id=1, source_target_pairs={{224,0},{228,4},{232,8},{236,12},{240,16},{244,20},{248,24},{252,2... | collective-permute-start | bytes 196616 | tf_op jit(solution)/shard_map/ppermute | solution.py:13
  560.5 7.5 %collective-permute-done.101 = bf16[8,4096]{1,0:T(8,128)(2,1)S(1)} collective-permute-done((bf16[8,4096]{1,0:T(8,128)(2,1)S(1)}, bf16[8,4096]{1,0:T(8,128)(2,1)S(1)}, u32[]{:S(2)}, u32[]{:S(2)}) %collective-permute-start.101) | collective-permute-done | bytes 65568 | tf_op jit(solution)/shard_map/ppermute | solution.py:13
  571.2 10.0 %collective-permute-start.103 = (bf16[8,4096]{1,0:T(8,128)(2,1)S(1)}, bf16[8,4096]{1,0:T(8,128)(2,1)S(1)}, u32[]{:S(2)}, u32[]{:S(2)}) collective-permute-start(bf16[8,4096]{1,0:T(8,128)(2,1)S(1)} %broadcast_select_fusion.3), channel_id=1, source_target_pairs={{32,64},{36,68},{40,72},{44,76},{48,80},{52,84},{56,88},{60,92},{1... | collective-permute-start | bytes 196616 | tf_op jit(solution)/shard_map/ppermute | solution.py:13
  581.2 15.5 %collective-permute-start.104 = (bf16[8,4096]{1,0:T(8,128)(2,1)S(1)}, bf16[8,4096]{1,0:T(8,128)(2,1)S(1)}, u32[]{:S(2)}, u32[]{:S(2)}) collective-permute-start(bf16[8,4096]{1,0:T(8,128)(2,1)S(1)} %get-tuple-element.10), channel_id=1, source_target_pairs={{0,8},{4,12},{8,0},{12,4},{16,24},{20,28},{24,16},{28,20},{32,40},... | collective-permute-start | bytes 196616 | tf_op jit(solution)/shard_map/ppermute | solution.py:13
  596.7 11.8 %collective-permute-start.105 = (bf16[8,4096]{1,0:T(8,128)(2,1)S(1)}, bf16[8,4096]{1,0:T(8,128)(2,1)S(1)}, u32[]{:S(2)}, u32[]{:S(2)}) collective-permute-start(bf16[8,4096]{1,0:T(8,128)(2,1)S(1)} %get-tuple-element.10), channel_id=1, source_target_pairs={{0,16},{4,20},{8,24},{12,28},{16,0},{20,4},{24,8},{28,12},{32,48},... | collective-permute-start | bytes 196616 | tf_op jit(solution)/shard_map/ppermute | solution.py:13
  608.6 11.8 %collective-permute-start.106 = (bf16[8,4096]{1,0:T(8,128)(2,1)S(1)}, bf16[8,4096]{1,0:T(8,128)(2,1)S(1)}, u32[]{:S(2)}, u32[]{:S(2)}) collective-permute-start(bf16[8,4096]{1,0:T(8,128)(2,1)S(1)} %get-tuple-element.10), channel_id=1, source_target_pairs={{0,24},{4,28},{8,16},{12,20},{16,8},{20,12},{24,0},{28,4},{32,56},... | collective-permute-start | bytes 196616 | tf_op jit(solution)/shard_map/ppermute | solution.py:13
  620.5 3.8 collective-permute-done.106
  624.3 11.0 %collective-permute-start.107 = (bf16[32,4096]{1,0:T(8,128)(2,1)S(1)}, bf16[32,4096]{1,0:T(8,128)(2,1)S(1)}, u32[]{:S(2)}, u32[]{:S(2)}) collective-permute-start(bf16[32,4096]{1,0:T(8,128)(2,1)S(1)} %pad_maximum_fusion.3), channel_id=1, source_target_pairs={{0,4},{4,0},{8,12},{12,8},{16,20},{20,16},{24,28},{28,24},{32,36},... | collective-permute-start | bytes 786440 | tf_op jit(solution)/shard_map/ppermute | solution.py:13
  638.7 11.2 %all-to-all-start = ((f32[64,1,128]{2,1,0:T(1,128)}), f32[64,1,128]{2,1,0:T(1,128)S(1)}, u32[]{:S(2)}, u32[]{:S(2)}) async-start(f32[64,1,128]{2,1,0:T(1,128)} %broadcast_in_dim.166), calls=%async_computation | async-start | bytes 65536 | tf_op jit(solution)/shard_map/all_to_all | solution.py:220
  650.6 7.9 %all-to-all-done = f32[64,1,128]{2,1,0:T(1,128)S(1)} async-done(((f32[64,1,128]{2,1,0:T(1,128)}), f32[64,1,128]{2,1,0:T(1,128)S(1)}, u32[]{:S(2)}, u32[]{:S(2)}) %all-to-all-start) | async-done | bytes 32800 | tf_op jit(solution)/shard_map/all_to_all | solution.py:220
  661.0 5.3 collective-permute-start.108
  666.3 3.1 collective-permute-done.108
  670.7 12.9 %collective-permute-start.109 = (f32[1,1]{1,0:T(1,128)}, f32[1,1]{1,0:T(1,128)}, u32[]{:S(2)}, u32[]{:S(2)}) collective-permute-start(f32[1,1]{1,0:T(1,128)} %add.858), channel_id=1, source_target_pairs={{0,3},{1,2},{2,1},{3,0},{4,7},{5,6},{6,5},{7,4},{8,11},{9,10},{10,... | collective-permute-start | bytes 20 | tf_op jit(solution)/shard_map/ppermute | solution.py:229
  (525 shorter events, 190.2 us)
Async XLA Ops:
  7.0 52.9 %collective-permute-start.48 = (bf16[2,32,64]{2,1,0:T(8,128)(2,1)S(1)}, bf16[2,32,64]{2,1,0:T(8,128)(2,1)}, u32[]{:S(2)}, u32[]{:S(2)}) collective-permute-start(bf16[2,32,64]{2,1,0:T(8,128)(2,1)S(1)} %convolution_convert_fusion.29), channel_id=1, source_target_pairs={{0,192},{4,196},{8,200},{12,204},{16,208},{20,212},{24,216},{28,22... | collective-permute-start | bytes 24584 | tf_op jit(solution)/shard_map/ppermute | solution.py:13
  15.8 53.0 %collective-permute-start.47 = (bf16[2,32,64]{2,1,0:T(8,128)(2,1)S(1)}, bf16[2,32,64]{2,1,0:T(8,128)(2,1)}, u32[]{:S(2)}, u32[]{:S(2)}) collective-permute-start(bf16[2,32,64]{2,1,0:T(8,128)(2,1)S(1)} %convolution_convert_fusion.29), channel_id=1, source_target_pairs={{64,192},{68,196},{72,200},{76,204},{80,208},{84,212},{88,216},{92... | collective-permute-start | bytes 24584 | tf_op jit(solution)/shard_map/ppermute | solution.py:13
  17.1 52.5 %collective-permute-start.46 = (bf16[2,32,64]{2,1,0:T(8,128)(2,1)S(1)}, bf16[2,32,64]{2,1,0:T(8,128)(2,1)}, u32[]{:S(2)}, u32[]{:S(2)}) collective-permute-start(bf16[2,32,64]{2,1,0:T(8,128)(2,1)S(1)} %convolution_convert_fusion.29), channel_id=1, source_target_pairs={{128,192},{132,196},{136,200},{140,204},{144,208},{148,212},{152,2... | collective-permute-start | bytes 24584 | tf_op jit(solution)/shard_map/ppermute | solution.py:13
  44.1 26.9 %collective-permute-start.49 = (bf16[64,4096]{1,0:T(8,128)(2,1)}, bf16[64,4096]{1,0:T(8,128)(2,1)}, u32[]{:S(2)}, u32[]{:S(2)}) collective-permute-start(bf16[64,4096]{1,0:T(8,128)(2,1)} %convolution_convert_fusion.3), channel_id=1, source_target_pairs={{0,4},{4,0},{8,12},{12,8},{16,20},{20,16},{24,28},{28,24},{32,36},... | collective-permute-start | bytes 1572872 | tf_op jit(solution)/shard_map/ppermute | solution.py:13
  47.2 319.1 %collective-permute-start.2 = (bf16[2,64,4096]{2,1,0:T(8,128)(2,1)}, bf16[2,64,4096]{2,1,0:T(8,128)(2,1)}, u32[]{:S(2)}, u32[]{:S(2)}) collective-permute-start(bf16[2,64,4096]{2,1,0:T(8,128)(2,1)} %slice.457), channel_id=1, source_target_pairs={{0,192},{4,196},{8,200},{12,204},{16,208},{20,212},{24,216},{28,22... | collective-permute-start | bytes 3145736 | tf_op jit(solution)/shard_map/ppermute | solution.py:13
  60.0 306.3 %collective-permute-start.1 = (bf16[2,64,4096]{2,1,0:T(8,128)(2,1)}, bf16[2,64,4096]{2,1,0:T(8,128)(2,1)}, u32[]{:S(2)}, u32[]{:S(2)}) collective-permute-start(bf16[2,64,4096]{2,1,0:T(8,128)(2,1)} %slice.457), channel_id=1, source_target_pairs={{64,192},{68,196},{72,200},{76,204},{80,208},{84,212},{88,216},{92... | collective-permute-start | bytes 3145736 | tf_op jit(solution)/shard_map/ppermute | solution.py:13
  68.9 12.2 %collective-permute-start.92 = (bf16[64,4096]{1,0:T(8,128)(2,1)S(1)}, bf16[64,4096]{1,0:T(8,128)(2,1)S(1)}, u32[]{:S(2)}, u32[]{:S(2)}) collective-permute-start(bf16[64,4096]{1,0:T(8,128)(2,1)S(1)} %copy-done.10), channel_id=1, source_target_pairs={{128,192},{132,196},{136,200},{140,204},{144,208},{148,212},{152,2... | collective-permute-start | bytes 1572872 | tf_op jit(solution)/shard_map/ppermute | solution.py:13
  69.6 15.2 %collective-permute-start.93 = (bf16[64,4096]{1,0:T(8,128)(2,1)S(1)}, bf16[64,4096]{1,0:T(8,128)(2,1)S(1)}, u32[]{:S(2)}, u32[]{:S(2)}) collective-permute-start(bf16[64,4096]{1,0:T(8,128)(2,1)S(1)} %copy-done.10), channel_id=1, source_target_pairs={{64,192},{68,196},{72,200},{76,204},{80,208},{84,212},{88,216},{92... | collective-permute-start | bytes 1572872 | tf_op jit(solution)/shard_map/ppermute | solution.py:13
  74.9 75.8 %collective-permute-start.94 = (bf16[64,4096]{1,0:T(8,128)(2,1)S(1)}, bf16[64,4096]{1,0:T(8,128)(2,1)S(1)}, u32[]{:S(2)}, u32[]{:S(2)}) collective-permute-start(bf16[64,4096]{1,0:T(8,128)(2,1)S(1)} %copy-done.10), channel_id=1, source_target_pairs={{0,192},{4,196},{8,200},{12,204},{16,208},{20,212},{24,216},{28,22... | collective-permute-start | bytes 1572872 | tf_op jit(solution)/shard_map/ppermute | solution.py:13
  81.1 72.0 %collective-permute-start.52 = (bf16[16,4096]{1,0:T(8,128)(2,1)S(1)}, bf16[16,4096]{1,0:T(8,128)(2,1)S(1)}, u32[]{:S(2)}, u32[]{:S(2)}) collective-permute-start(bf16[16,4096]{1,0:T(8,128)(2,1)S(1)} %get-tuple-element.69), channel_id=1, source_target_pairs={{0,24},{4,28},{8,16},{12,20},{16,8},{20,12},{24,0},{28,4},{32,56},... | collective-permute-start | bytes 393224 | tf_op jit(solution)/shard_map/ppermute | solution.py:13
  84.7 72.7 %collective-permute-start.51 = (bf16[16,4096]{1,0:T(8,128)(2,1)S(1)}, bf16[16,4096]{1,0:T(8,128)(2,1)S(1)}, u32[]{:S(2)}, u32[]{:S(2)}) collective-permute-start(bf16[16,4096]{1,0:T(8,128)(2,1)S(1)} %get-tuple-element.70), channel_id=1, source_target_pairs={{0,16},{4,20},{8,24},{12,28},{16,0},{20,4},{24,8},{28,12},{32,48},... | collective-permute-start | bytes 393224 | tf_op jit(solution)/shard_map/ppermute | solution.py:13
  150.7 9.9 %collective-permute-start.50 = (bf16[16,4096]{1,0:T(8,128)(2,1)S(1)}, bf16[16,4096]{1,0:T(8,128)(2,1)S(1)}, u32[]{:S(2)}, u32[]{:S(2)}) collective-permute-start(bf16[16,4096]{1,0:T(8,128)(2,1)S(1)} %get-tuple-element.68), channel_id=1, source_target_pairs={{0,8},{4,12},{8,0},{12,4},{16,24},{20,28},{24,16},{28,20},{32,40},... | collective-permute-start | bytes 393224 | tf_op jit(solution)/shard_map/ppermute | solution.py:13
  153.1 10.4 %collective-permute-start.6 = (bf16[16,4096]{1,0:T(8,128)(2,1)S(1)}, bf16[16,4096]{1,0:T(8,128)(2,1)S(1)}, u32[]{:S(2)}, u32[]{:S(2)}) collective-permute-start(bf16[16,4096]{1,0:T(8,128)(2,1)S(1)} %get-tuple-element.81), channel_id=1, source_target_pairs={{0,24},{4,28},{8,16},{12,20},{16,8},{20,12},{24,0},{28,4},{32,56},... | collective-permute-start | bytes 393224 | tf_op jit(solution)/shard_map/ppermute | solution.py:13
  157.4 9.0 %collective-permute-start.5 = (bf16[16,4096]{1,0:T(8,128)(2,1)S(1)}, bf16[16,4096]{1,0:T(8,128)(2,1)S(1)}, u32[]{:S(2)}, u32[]{:S(2)}) collective-permute-start(bf16[16,4096]{1,0:T(8,128)(2,1)S(1)} %get-tuple-element.82), channel_id=1, source_target_pairs={{0,16},{4,20},{8,24},{12,28},{16,0},{20,4},{24,8},{28,12},{32,48},... | collective-permute-start | bytes 393224 | tf_op jit(solution)/shard_map/ppermute | solution.py:13
  186.8 9.4 %collective-permute-start.13 = (bf16[64,4096]{1,0:T(8,128)(2,1)}, bf16[64,4096]{1,0:T(8,128)(2,1)}, u32[]{:S(2)}, u32[]{:S(2)}) collective-permute-start(bf16[64,4096]{1,0:T(8,128)(2,1)} %get-tuple-element.161), channel_id=1, source_target_pairs={{64,68},{68,64},{72,76},{76,72},{80,84},{84,80},{88,92},{92,88},{9... | collective-permute-start | bytes 1572872 | tf_op jit(solution)/shard_map/ppermute | solution.py:13
  194.7 9.5 %collective-permute-start.60 = (bf16[64,4096]{1,0:T(8,128)(2,1)}, bf16[64,4096]{1,0:T(8,128)(2,1)}, u32[]{:S(2)}, u32[]{:S(2)}) collective-permute-start(bf16[64,4096]{1,0:T(8,128)(2,1)} %convolution_convert_fusion.2), channel_id=1, source_target_pairs={{64,68},{68,64},{72,76},{76,72},{80,84},{84,80},{88,92},{92,88},{9... | collective-permute-start | bytes 1572872 | tf_op jit(solution)/shard_map/ppermute | solution.py:13
  211.5 58.2 %collective-permute-start.18 = (bf16[8,4096]{1,0:T(8,128)(2,1)S(1)}, bf16[8,4096]{1,0:T(8,128)(2,1)S(1)}, u32[]{:S(2)}, u32[]{:S(2)}) collective-permute-start(bf16[8,4096]{1,0:T(8,128)(2,1)S(1)} %slice.835), channel_id=1, source_target_pairs={{64,96},{68,100},{72,104},{76,108},{80,112},{84,116},{88,120},{92,... | collective-permute-start | bytes 196616 | tf_op jit(solution)/shard_map/ppermute | solution.py:13
  212.2 70.0 %collective-permute-start.65 = (bf16[8,4096]{1,0:T(8,128)(2,1)S(1)}, bf16[8,4096]{1,0:T(8,128)(2,1)S(1)}, u32[]{:S(2)}, u32[]{:S(2)}) collective-permute-start(bf16[8,4096]{1,0:T(8,128)(2,1)S(1)} %fusion.97), channel_id=1, source_target_pairs={{64,128},{68,132},{72,136},{76,140},{80,144},{84,148},{88,152},{92... | collective-permute-start | bytes 196616 | tf_op jit(solution)/shard_map/ppermute | solution.py:13
  269.7 12.6 %collective-permute-start.19 = (bf16[8,4096]{1,0:T(8,128)(2,1)S(1)}, bf16[8,4096]{1,0:T(8,128)(2,1)S(1)}, u32[]{:S(2)}, u32[]{:S(2)}) collective-permute-start(bf16[8,4096]{1,0:T(8,128)(2,1)S(1)} %fusion.85), channel_id=1, source_target_pairs={{64,128},{68,132},{72,136},{76,140},{80,144},{84,148},{88,152},{92... | collective-permute-start | bytes 196616 | tf_op jit(solution)/shard_map/ppermute | solution.py:13
  292.2 9.6 %collective-permute-start.24 = (bf16[64,4096]{1,0:T(8,128)(2,1)}, bf16[64,4096]{1,0:T(8,128)(2,1)}, u32[]{:S(2)}, u32[]{:S(2)}) collective-permute-start(bf16[64,4096]{1,0:T(8,128)(2,1)} %get-tuple-element.150), channel_id=1, source_target_pairs={{128,132},{132,128},{136,140},{140,136},{144,148},{148,144},{152,1... | collective-permute-start | bytes 1572872 | tf_op jit(solution)/shard_map/ppermute | solution.py:13
  300.2 9.7 %collective-permute-start.71 = (bf16[64,4096]{1,0:T(8,128)(2,1)}, bf16[64,4096]{1,0:T(8,128)(2,1)}, u32[]{:S(2)}, u32[]{:S(2)}) collective-permute-start(bf16[64,4096]{1,0:T(8,128)(2,1)} %convolution_convert_fusion.1), channel_id=1, source_target_pairs={{128,132},{132,128},{136,140},{140,136},{144,148},{148,144},{152,1... | collective-permute-start | bytes 1572872 | tf_op jit(solution)/shard_map/ppermute | solution.py:13
  329.4 9.4 %collective-permute-start.35 = (bf16[64,4096]{1,0:T(8,128)(2,1)}, bf16[64,4096]{1,0:T(8,128)(2,1)}, u32[]{:S(2)}, u32[]{:S(2)}) collective-permute-start(bf16[64,4096]{1,0:T(8,128)(2,1)} %get-tuple-element.144), channel_id=1, source_target_pairs={{192,196},{196,192},{200,204},{204,200},{208,212},{212,208},{216,2... | collective-permute-start | bytes 1572872 | tf_op jit(solution)/shard_map/ppermute | solution.py:13
  337.3 9.5 %collective-permute-start.82 = (bf16[64,4096]{1,0:T(8,128)(2,1)}, bf16[64,4096]{1,0:T(8,128)(2,1)}, u32[]{:S(2)}, u32[]{:S(2)}) collective-permute-start(bf16[64,4096]{1,0:T(8,128)(2,1)} %convolution_convert_fusion), channel_id=1, source_target_pairs={{192,196},{196,192},{200,204},{204,200},{208,212},{212,208},{216,2... | collective-permute-start | bytes 1572872 | tf_op jit(solution)/shard_map/ppermute | solution.py:13
  353.0 13.2 %collective-permute-start = (bf16[2,64,4096]{2,1,0:T(8,128)(2,1)}, bf16[2,64,4096]{2,1,0:T(8,128)(2,1)S(1)}, u32[]{:S(2)}, u32[]{:S(2)}) collective-permute-start(bf16[2,64,4096]{2,1,0:T(8,128)(2,1)} %slice.457), channel_id=1, source_target_pairs={{128,192},{132,196},{136,200},{140,204},{144,208},{148,212},{152,2... | collective-permute-start | bytes 3145736 | tf_op jit(solution)/shard_map/ppermute | solution.py:13
  384.8 183.1 %collective-permute-start.101 = (bf16[8,4096]{1,0:T(8,128)(2,1)S(1)}, bf16[8,4096]{1,0:T(8,128)(2,1)S(1)}, u32[]{:S(2)}, u32[]{:S(2)}) collective-permute-start(bf16[8,4096]{1,0:T(8,128)(2,1)S(1)} %pad_maximum_fusion.13), channel_id=1, source_target_pairs={{224,0},{228,4},{232,8},{236,12},{240,16},{244,20},{248,24},{252,2... | collective-permute-start | bytes 196616 | tf_op jit(solution)/shard_map/ppermute | solution.py:13
  571.2 10.0 %collective-permute-start.103 = (bf16[8,4096]{1,0:T(8,128)(2,1)S(1)}, bf16[8,4096]{1,0:T(8,128)(2,1)S(1)}, u32[]{:S(2)}, u32[]{:S(2)}) collective-permute-start(bf16[8,4096]{1,0:T(8,128)(2,1)S(1)} %broadcast_select_fusion.3), channel_id=1, source_target_pairs={{32,64},{36,68},{40,72},{44,76},{48,80},{52,84},{56,88},{60,92},{1... | collective-permute-start | bytes 196616 | tf_op jit(solution)/shard_map/ppermute | solution.py:13
  581.2 39.2 %collective-permute-start.104 = (bf16[8,4096]{1,0:T(8,128)(2,1)S(1)}, bf16[8,4096]{1,0:T(8,128)(2,1)S(1)}, u32[]{:S(2)}, u32[]{:S(2)}) collective-permute-start(bf16[8,4096]{1,0:T(8,128)(2,1)S(1)} %get-tuple-element.10), channel_id=1, source_target_pairs={{0,8},{4,12},{8,0},{12,4},{16,24},{20,28},{24,16},{28,20},{32,40},... | collective-permute-start | bytes 196616 | tf_op jit(solution)/shard_map/ppermute | solution.py:13
  596.7 23.7 %collective-permute-start.105 = (bf16[8,4096]{1,0:T(8,128)(2,1)S(1)}, bf16[8,4096]{1,0:T(8,128)(2,1)S(1)}, u32[]{:S(2)}, u32[]{:S(2)}) collective-permute-start(bf16[8,4096]{1,0:T(8,128)(2,1)S(1)} %get-tuple-element.10), channel_id=1, source_target_pairs={{0,16},{4,20},{8,24},{12,28},{16,0},{20,4},{24,8},{28,12},{32,48},... | collective-permute-start | bytes 196616 | tf_op jit(solution)/shard_map/ppermute | solution.py:13
  608.6 15.7 %collective-permute-start.106 = (bf16[8,4096]{1,0:T(8,128)(2,1)S(1)}, bf16[8,4096]{1,0:T(8,128)(2,1)S(1)}, u32[]{:S(2)}, u32[]{:S(2)}) collective-permute-start(bf16[8,4096]{1,0:T(8,128)(2,1)S(1)} %get-tuple-element.10), channel_id=1, source_target_pairs={{0,24},{4,28},{8,16},{12,20},{16,8},{20,12},{24,0},{28,4},{32,56},... | collective-permute-start | bytes 196616 | tf_op jit(solution)/shard_map/ppermute | solution.py:13
  624.3 12.1 %collective-permute-start.107 = (bf16[32,4096]{1,0:T(8,128)(2,1)S(1)}, bf16[32,4096]{1,0:T(8,128)(2,1)S(1)}, u32[]{:S(2)}, u32[]{:S(2)}) collective-permute-start(bf16[32,4096]{1,0:T(8,128)(2,1)S(1)} %pad_maximum_fusion.3), channel_id=1, source_target_pairs={{0,4},{4,0},{8,12},{12,8},{16,20},{20,16},{24,28},{28,24},{32,36},... | collective-permute-start | bytes 786440 | tf_op jit(solution)/shard_map/ppermute | solution.py:13
  638.7 19.8 %all-to-all-start = ((f32[64,1,128]{2,1,0:T(1,128)}), f32[64,1,128]{2,1,0:T(1,128)S(1)}, u32[]{:S(2)}, u32[]{:S(2)}) async-start(f32[64,1,128]{2,1,0:T(1,128)} %broadcast_in_dim.166), calls=%async_computation | async-start | bytes 65536 | tf_op jit(solution)/shard_map/all_to_all | solution.py:220
  670.7 15.8 %collective-permute-start.109 = (f32[1,1]{1,0:T(1,128)}, f32[1,1]{1,0:T(1,128)}, u32[]{:S(2)}, u32[]{:S(2)}) collective-permute-start(f32[1,1]{1,0:T(1,128)} %add.858), channel_id=1, source_target_pairs={{0,3},{1,2},{2,1},{3,0},{4,7},{5,6},{6,5},{7,4},{8,11},{9,10},{10,... | collective-permute-start | bytes 20 | tf_op jit(solution)/shard_map/ppermute | solution.py:229
  (115 other events, 1565.6 us)
